TPU v7x, 32 devices: a whole 2x2x4 slice. The times are simulated.
32 devices in a mesh: dp: 8 (over y, x, core), fsdp: 4 (over z).
Axes of the slice: x: 2, y: 2, z: 4, core: 2. Of those that a mesh axis runs over, the one named last changes fastest.
Arguments:
- tokens: bfloat16 [32768, 768], P(('dp', 'fsdp')), may hold values from -6 to 6
- lengths: int32 [32], P(('dp', 'fsdp')), may hold values from 1 to 1024, 24576 in all
- cotangent: bfloat16 [32768, 768], P(('dp', 'fsdp')), may hold values from -6 to 6
- project_weight: bfloat16 [768, 2304], P('dp', 'fsdp'), may hold values from -0.21875 to 0.21875
- project_bias: bfloat16 [1536], P('dp'), may hold values from -1.1953125 to 1.1953125
- output_weight: bfloat16 [768, 768], P('dp', 'fsdp'), may hold values from -3.5 to 3.5
- output_bias: bfloat16 [768], P('dp'), may hold values from -1.1953125 to 1.1953125
- expand_weight: bfloat16 [768, 3072], P('dp', 'fsdp'), may hold values from -0.21875 to 0.21875
- expand_bias: bfloat16 [3072], P('dp'), may hold values from -1.1953125 to 1.1953125
- contract_weight: bfloat16 [3072, 768], P('dp', 'fsdp'), may hold values from -0.109375 to 0.109375
- contract_bias: bfloat16 [768], P('dp'), may hold values from -1.1953125 to 1.1953125
- first_gain: bfloat16 [768], P('dp'), may hold values from 0.25 to 1.75
- first_shift: bfloat16 [768], P('dp'), may hold values from -1.1953125 to 1.1953125
- second_gain: bfloat16 [768], P('dp'), may hold values from 0.25 to 1.75
- second_shift: bfloat16 [768], P('dp'), may hold values from -1.1953125 to 1.1953125
Outputs:
- block_out: bfloat16 [32768, 768], P(('dp', 'fsdp'))
- tokens_grad: bfloat16 [32768, 768], P(('dp', 'fsdp'))
- project_weight_grad: float32 [768, 2304], P('dp', 'fsdp')
- project_bias_grad: float32 [1536], P('dp')
- output_weight_grad: float32 [768, 768], P('dp', 'fsdp')
- output_bias_grad: float32 [768], P('dp')
- expand_weight_grad: float32 [768, 3072], P('dp', 'fsdp')
- expand_bias_grad: float32 [3072], P('dp')
- contract_weight_grad: float32 [3072, 768], P('dp', 'fsdp')
- contract_bias_grad: float32 [768], P('dp')
- first_gain_grad: float32 [768], P('dp')
- first_shift_grad: float32 [768], P('dp')
- second_gain_grad: float32 [768], P('dp')
- second_shift_grad: float32 [768], P('dp')
Inputs may be any that keep to these rules, and one draw needn't show every extreme that they name: `lengths`: each cell's number of live tokens; some cell has exactly 1024.
All inputs are finite; a program needn't handle non-finite values. No bound on the sum of `lengths` on one device may be relied on, other than what follows from the above.
Results may differ from a plain program's by a relative error of at most 0.013.
Values may be sent and summed in bfloat16 or wider, within the bound.
A program may use at most 256 MiB of HBM per device.

v0:
```python
import functools
import jax
import jax.numpy as jnp
from jax import lax
from jax.experimental import pallas as pl
from jax.experimental.pallas import tpu as pltpu
from jax.sharding import PartitionSpec as P

H = 12
HD = 64
F32 = jnp.float32
BF = jnp.bfloat16
MESH = pl.DeviceIdType.MESH
eps_norm = 1e-05
neg_fill = -1000000000.0


def dot(first, second):
    return jnp.dot(first, second, preferred_element_type=F32)


def dot_nt(first, second):
    return lax.dot_general(first, second, (((1,), (1,)), ((), ())), preferred_element_type=F32)


def dot_tn(first, second):
    return lax.dot_general(first, second, (((0,), (0,)), ((), ())), preferred_element_type=F32)


def mo(value, multiple):
    return pl.multiple_of(value, multiple)


class Place:
    def __init__(self):
        self.d = lax.axis_index("dp")
        self.z = lax.axis_index("fsdp")
        core = lax.rem(self.d, 2)
        across = lax.rem(lax.div(self.d, 2), 2)
        up = lax.div(self.d, 4)
        self.dc = self.d + 1 - 2 * core
        self.dx = self.d + 2 - 4 * across
        self.dy = self.d + 4 - 8 * up
        self.dd = self.dx + 4 - 8 * up
        self.odd = lax.rem(self.z, 2)
        z = self.z
        pick = lambda a, b, c, d: jnp.where(z < 2, jnp.where(z == 0, a, b), jnp.where(z == 2, c, d))
        self.order = [z, pick(1, 0, 3, 2), pick(2, 2, 1, 1), pick(3, 3, 0, 0)]

    def zt(self, step):
        return lax.rem(self.z + step, 4)

    def zf(self, step):
        return lax.rem(self.z + 4 - step, 4)

    def id(self, to):
        if to == "x":
            return (self.dx, self.z)
        if to == "y":
            return (self.dy, self.z)
        if to == "c":
            return (self.dc, self.z)
        if isinstance(to, tuple):
            return (to[1], self.z) if to[0] == "d" else (self.d, to[1])
        return (self.d, self.zt(to))


def enter(place, wide=False):
    barrier = pltpu.get_barrier_semaphore()
    sib = place.dc - place.d
    others = [("d", d + sib) for d in (place.dx, place.dy, place.dd)] + [("d", place.dd)] if wide else []
    partners = ["x", "y", "c", 1, 2, 3] + others
    for to in partners:
        pl.semaphore_signal(barrier, inc=1, device_id=place.id(to), device_id_type=MESH)
    pl.semaphore_wait(barrier, len(partners))


class Link:
    def __init__(self, place, send_sem, recv_sem):
        self.place, self.send_sem, self.recv_sem = place, send_sem, recv_sem
        self.count = 0
        self.copies = []

    def slot(self, many=1):
        self.count += many
        return self.count - many

    def copy(self, slot, source, target, to, land=None):
        return pltpu.make_async_remote_copy(
            src_ref=source, dst_ref=target, send_sem=self.send_sem.at[slot],
            recv_sem=self.recv_sem.at[slot if land is None else land], device_id=self.place.id(to),
            device_id_type=MESH)

    def send(self, slot, source, target, to, like, land=None, when=None):
        def start():
            self.copy(slot, source, target, to, land).start()

        if when is None:
            start()
        else:
            pl.when(when())(start)
        self.copies.append((slot, like, when))

    def got(self, slot, target):
        self.copy(slot, target, target, "x").wait_recv()

    def finish(self):
        for slot, like, when in self.copies:
            def done(slot=slot, like=like):
                view = like()
                self.copy(slot, view, view, "x").wait_send()

            if when is None:
                done()
            else:
                pl.when(when())(done)


class Gather:
    def __init__(self, link, place, block):
        p = place
        zr, zs = link.slot(4), link.slot(4)
        xs, ys, fx = link.slot(4), link.slot(4), link.slot(4)
        cs = link.slot(16)
        got = link.got
        send = functools.partial(link.send, like=lambda: block(0, 0))

        def z_step(a):
            def run():
                if a == 0:
                    own = block(p.z, p.d)
                    for k in (1, 2, 3):
                        send(zs + k, own, own, ("z", p.order[k]), land=zr + p.z)
                else:
                    got(zr + p.order[a], block(p.order[a], p.d))
            return run

        def x_step(a):
            def run():
                here = block(p.order[a], p.d)
                send(xs + a, here, here, "x")
                send(ys + a, here, here, "y")
                send(cs + a, here, here, "c")
            return run

        def turn(a):
            def run():
                b = p.order[a]
                bx, by = block(b, p.dx), block(b, p.dy)
                got(xs + a, bx)
                got(ys + a, by)
                if a in (0, 1):
                    send(fx + a, bx, bx, "y")
                else:
                    send(fx + a, by, by, "x")
                send(cs + 4 + a, bx, bx, "c")
                send(cs + 8 + a, by, by, "c")
            return run

        def corner(a):
            def run():
                bd = block(p.order[a], p.dd)
                got(fx + a, bd)
                send(cs + 12 + a, bd, bd, "c")
            return run

        def close():
            sib = p.dc - p.d
            for which, d in enumerate((p.d, p.dx, p.dy, p.dd)):
                for a in range(4):
                    got(cs + 4 * which + a, block(p.order[a], d + sib))

        self.z, self.x, self.t, self.q = ([make(a) for a in range(4)] for make in (z_step, x_step, turn, corner))
        self.close = close


def spread_z(link, place, ref):
    p = place
    zs, zr = link.slot(3), link.slot(4)

    def send():
        for k in (1, 2, 3):
            link.send(zs + k - 1, ref.at[p.z], ref.at[p.z], ("z", p.order[k]), lambda: ref.at[0], land=zr + p.z)

    def wait():
        for k in (1, 2, 3):
            b = p.order[k]
            link.got(zr + b, ref.at[b])

    return send, wait


def run(*events):
    def together():
        for event in events:
            event()
    return together


def window(value, odd, wide):
    rows, k = value.shape
    fill = jnp.zeros((rows, wide - k), F32)
    value = value.astype(F32)
    left = jnp.concatenate([value, fill], axis=1)
    right = jnp.concatenate([fill, value], axis=1)
    return jnp.where(odd == 0, left, right).astype(BF)


def merge_windows(blocks, full, tiles, rows_step):
    rows = full.shape[0]
    half = tiles // 2

    def body(i, _):
        r = pl.ds(mo(i * rows_step, rows_step), rows_step)
        for pair in range(2):
            even, odd = blocks.at[2 * pair], blocks.at[2 * pair + 1]
            base = pair * tiles * 128
            full[r, base:base + half * 128] = even[r, 0:half * 128]
            full[r, base + half * 128:base + (half + 1) * 128] = (
                even[r, half * 128:(half + 1) * 128] + odd[r, 0:128])
            full[r, base + (half + 1) * 128:base + tiles * 128] = odd[r, 128:(half + 1) * 128]
        return 0

    lax.fori_loop(0, rows // rows_step, body, 0)


def split3(value):
    high = value.astype(BF)
    rest = value - high.astype(F32)
    mid = rest.astype(BF)
    low = (rest - mid.astype(F32)).astype(BF)
    return high.astype(F32), mid.astype(F32), low.astype(F32)


def extend(head, pair, lane, one, two, three, four):
    base = 64 * (1 - head)
    extra = jnp.where(lane == base, one, jnp.where(lane == base + 1, two, jnp.where(
        lane == base + 2, three, jnp.where(lane == base + 3, four, 0.0))))
    keep = (lane < 64) if head == 0 else (lane >= 64)
    return jnp.where(keep, pair, extra).astype(BF)


def iota(shape, axis):
    return lax.broadcasted_iota(jnp.int32, shape, axis)


QB = 256


def first_kernel(length_ref, x_ref, wp_ref, wo_ref, we_ref, wc_ref, *refs):
    vec_refs, refs = refs[:8], refs[8:]
    first_body(length_ref, x_ref, wp_ref, wo_ref, we_ref, wc_ref, vec_refs, *refs)


def first_body(length_ref, x_ref, wp_ref, wo_ref, we_ref, wc_ref, vec_refs,
                 n1_out, proj_out, mixed_out, qa_out, wp_out, wo_out, we_out, c_out, v_out,
                 wp_blk, wo_blk, we, wp, wo, vb, n1, proj, mixed, qa, ka, va, vrow, cc,
                 send_sem, recv_sem, out_sem, pair_sem):
    p = Place()
    T, D = x_ref.shape
    R = wp_ref.shape[0]
    FF = we.shape[1]
    link = Link(p, send_sem, recv_sem)
    rows_of = lambda d: pl.ds(mo(d * R, 16), R)
    half = R // 2
    bpa = lambda z, d: wp_blk.at[z, pl.ds(mo(d * R, 16), half), :]
    bpb = lambda z, d: wp_blk.at[z, pl.ds(mo(d * R + half, 16), half), :]
    bo = lambda z, d: wo_blk.at[z, rows_of(d), :]
    be = lambda z, d: we.at[rows_of(d), pl.ds(mo(z * (FF // 4), 128), FF // 4)]
    g0, g1, go, ge = (Gather(link, p, b) for b in (bpa, bpb, bo, be))
    c_send, c_wait = spread_z(link, p, cc)
    vs = [link.slot() for _ in range(7)]

    wp_blk[p.z, rows_of(p.d), :] = window(wp_ref[...], p.odd, wp_blk.shape[2])
    wo_blk[p.z, rows_of(p.d), :] = window(wo_ref[...], p.odd, wo_blk.shape[2])
    we[rows_of(p.d), pl.ds(mo(p.z * (FF // 4), 128), FF // 4)] = we_ref[...]
    cc[p.z] = wc_ref[...]
    for i, ref in enumerate(vec_refs):
        vb[p.d, i:i + 1, 0:ref.shape[0]] = ref[...].astype(F32).reshape(1, ref.shape[0]).astype(BF)

    outs = []

    def out(source, target):
        made = pltpu.make_async_copy(source, target, out_sem.at[len(outs)])
        made.start()
        outs.append(made)

    enter(p)
    send_v = lambda slot, d, to: link.send(vs[slot], vb.at[d], vb.at[d], to, lambda: vb.at[0])
    for slot, to in ((0, "x"), (1, "y"), (3, "c")):
        send_v(slot, p.d, to)
    run(g0.z[0], g0.x[0], g1.z[0], g1.x[0])()
    link.got(vs[0], vb.at[p.dx])
    link.got(vs[1], vb.at[p.dy])
    send_v(2, p.dx, "y")
    send_v(4, p.dx, "c")
    send_v(5, p.dy, "c")
    run(g0.z[1], g0.x[1], g0.t[0], g1.t[0], g0.z[2], g0.x[2])()
    link.got(vs[2], vb.at[p.dd])
    send_v(6, p.dd, "c")
    sib = p.dc - p.d
    for slot, d in ((3, p.d), (4, p.dx), (5, p.dy), (6, p.dd)):
        link.got(vs[slot], vb.at[d + sib])
    got = vb[...].astype(F32)
    side = lambda row, wide: jnp.concatenate([got[i, row:row + 1, 0:wide] for i in range(8)], axis=1)
    bias = side(0, 2 * R)
    vrow[0:1, 0:D] = bias[:, 0:D]
    vrow[0:1, D:2 * D] = jnp.zeros((1, D), F32)
    vrow[0:1, 2 * D:3 * D] = bias[:, D:]
    vrow[1:2, :] = side(2, FF // 8)
    for row, at in ((2, 1), (3, 3), (4, 4), (5, 5), (6, 6), (7, 7)):
        vrow[row:row + 1, 0:D] = side(at, R)
    out(vrow, v_out)
    run(g0.t[1], g0.z[3], g0.x[3], g0.q[0], g1.z[1], g1.x[1], g1.q[0])()

    LR = 128
    gain, shift = vrow[4:5, 0:D], vrow[5:6, 0:D]

    def norm_body(i, _):
        r = pl.ds(mo(i * LR, LR), LR)
        value = x_ref[r, :].astype(F32)
        u = value - jnp.mean(value, axis=-1, keepdims=True)
        spread = jnp.mean(u * u, axis=-1, keepdims=True)
        n1[r, :] = (u * lax.rsqrt(spread + eps_norm) * gain + shift).astype(BF)
        return 0

    norm_part = lambda k: lax.fori_loop(k * (T // LR // 4), (k + 1) * (T // LR // 4), norm_body, 0)
    g0.t[2]()
    norm_part(0)
    run(g1.z[2], g1.x[2], g0.q[1])()
    norm_part(1)
    run(g1.z[3], g1.x[3], ge.z[0], go.z[0], g0.t[3])()
    norm_part(2)
    run(g0.q[2], g1.t[1])()
    norm_part(3)
    run(g1.t[2], g1.t[3], ge.x[0], g0.q[3], g1.q[1], g1.q[2], g1.q[3], go.x[0])()
    out(n1, n1_out)
    run(g0.close, g1.close)()
    merge_windows(wp_blk, wp, 9, 96)
    out(wp, wp_out)
    run(ge.z[1], ge.x[1])()

    def project_body(i, _):
        for at, event in ((2, run(ge.z[2], ge.x[2], ge.t[0])), (3, go.t[0])):
            pl.when(i == at)(event)
        r = pl.ds(mo(i * 256, 256), 256)
        left = n1[r, :]
        for j in range(3):
            cols = slice(j * D, (j + 1) * D)
            value = dot(left, wp[:, cols]) + vrow[0:1, cols]
            proj[r, cols] = value.astype(BF)
        return 0

    lax.fori_loop(0, T // 256, project_body, 0)
    out(proj, proj_out)

    length = length_ref[0]
    subs = T // QB

    def pair_outs(pair):
        heads = pl.ds(2 * pair, 2)
        cols = pl.ds(mo(pair * 128, 128), 128)
        return (pltpu.make_async_copy(qa.at[heads], qa_out.at[heads], pair_sem.at[pair, 0]),
                pltpu.make_async_copy(mixed.at[:, cols], mixed_out.at[:, cols], pair_sem.at[pair, 1]))

    def attend_steps(events):
        def body(pair, _):
            for at, event in events:
                pl.when(pair == at)(event)
            cols = lambda off: pl.ds(mo(off + pair * 128, 128), 128)
            lane, row = iota((T, 128), 1), iota((T, 128), 0)
            q = proj[:, cols(0)].astype(F32) * (HD ** -0.5)
            k = proj[:, cols(D)].astype(F32)
            v = proj[:, cols(2 * D)].astype(F32)
            dead = jnp.where(row < length, 0.0, neg_fill)
            for head in range(2):
                ka[head] = extend(head, k, lane, 1.0, 1.0, 1.0, dead)
                qa[pair * 2 + head] = extend(head, q, lane, 0.0, 0.0, 0.0, 1.0)
                keep = (lane < 64) if head == 0 else (lane >= 64)
                va[head] = jnp.where(keep, v, 1.0).astype(BF)
            sub_lane = iota((QB, 128), 1)
            items = [(head, pl.ds(i * QB, QB)) for i in range(subs) for head in range(2)]
            halves = {}

            def scores(n):
                head, r = items[n]
                return dot_nt(qa[pair * 2 + head, r, :], ka[head])

            def soften(value):
                top = jnp.max(value, axis=-1, keepdims=True)
                return top, jnp.exp(value - top).astype(BF)

            def finish(n, top, powers):
                head, r = items[n]
                value = dot(powers, va[head])
                total = value[:, 64:65] if head == 0 else value[:, 0:1]
                one, two, three = split3(-(top + jnp.log(total)))
                query = qa[pair * 2 + head, r, :].astype(F32)
                qa[pair * 2 + head, r, :] = extend(head, query, sub_lane, one, two, three, 1.0)
                halves[n] = value * (1.0 / total)
                if head == 1:
                    mixed[r, cols(0)] = jnp.where(sub_lane < 64, halves[n - 1], halves[n]).astype(BF)

            value, waiting = scores(0), None
            for n in range(len(items)):
                following = scores(n + 1) if n + 1 < len(items) else None
                soft = soften(value)
                if waiting is not None:
                    finish(n - 1, *waiting)
                value, waiting = following, soft
            finish(len(items) - 1, *waiting)
            for made in pair_outs(pair):
                made.start()
            return 0

        lax.fori_loop(0, H // 2, body, 0)

    attend_steps([(1, run(go.z[1], go.x[1], ge.z[3], ge.x[3], go.z[2], go.x[2], ge.t[1])),
                  (2, run(go.z[3], go.x[3], ge.t[2], c_send)), (3, run(ge.q[0], go.t[1], go.q[0])),
                  (4, run(ge.t[3], go.t[2])), (5, run(ge.q[1], ge.q[2], go.t[3]))])
    run(ge.q[3], go.q[1], go.q[2], go.q[3], go.close)()
    merge_windows(wo_blk, wo, 3, 96)
    out(wo, wo_out)
    ge.close()
    out(we, we_out)
    c_wait()
    out(cc, c_out)
    link.finish()
    for made in outs:
        made.wait()
    for pair in range(H // 2):
        for made in pair_outs(pair):
            made.wait()


def first_call(length, x, wp, wo, we, wc, vectors):
    T, D = x.shape
    FF = we.shape[1] * 4
    ANY = pl.BlockSpec(memory_space=pl.ANY)
    V = pl.BlockSpec(memory_space=pltpu.VMEM)
    S = pl.BlockSpec(memory_space=pltpu.SMEM)
    sds = jax.ShapeDtypeStruct
    n = 4 * 36 + 7 + 7
    return pl.pallas_call(
        first_kernel,
        in_specs=[S] + [V] * 13,
        out_specs=[ANY] * 9,
        out_shape=[sds((T, D), BF), sds((T, 3 * D), BF), sds((T, D), BF), sds((H, T, 128), BF),
                   sds((D, 3 * D), BF), sds((D, D), BF), sds((D, FF), BF), sds((4,) + wc.shape, BF), sds((8, FF), F32)],
        scratch_shapes=[
            pltpu.VMEM((4, D, 640), BF), pltpu.VMEM((4, D, 256), BF), pltpu.VMEM((D, FF), BF),
            pltpu.VMEM((D, 3 * D), BF), pltpu.VMEM((D, D), BF), pltpu.VMEM((8, 16, FF // 8), BF),
            pltpu.VMEM((T, D), BF), pltpu.VMEM((T, 3 * D), BF), pltpu.VMEM((T, D), BF),
            pltpu.VMEM((H, T, 128), BF), pltpu.VMEM((2, T, 128), BF), pltpu.VMEM((2, T, 128), BF),
            pltpu.VMEM((8, FF), F32), pltpu.VMEM((4,) + wc.shape, BF),
            pltpu.SemaphoreType.DMA((n,)), pltpu.SemaphoreType.DMA((n,)), pltpu.SemaphoreType.DMA((9,)), pltpu.SemaphoreType.DMA((H // 2, 2)),
        ],
        compiler_params=pltpu.CompilerParams(
            collective_id=0, has_side_effects=True, vmem_limit_bytes=60 << 20),
        name="first_part",
    )(length, x, wp, wo, we, wc, *vectors)


def layer_norm(values, gain_row, shift_row):
    centre = jnp.mean(values, axis=-1, keepdims=True)
    centred = values - centre
    spread = jnp.mean(centred * centred, axis=-1, keepdims=True)
    return centred * lax.rsqrt(spread + eps_norm) * gain_row + shift_row


def gelu_exact(values):
    return jax.nn.gelu(values, approximate=False)


def matmul(first, second):
    return jnp.dot(first, second, preferred_element_type=jnp.float32)


def over_rows(first, second):
    return lax.dot_general(
        first, second, (((0,), (0,)), ((), ())), preferred_element_type=jnp.float32
    )


def over_columns(first, second):
    return lax.dot_general(
        first, second, (((1,), (1,)), ((), ())), preferred_element_type=jnp.float32
    )


def fetch_forward(
    project_weight,
    output_weight,
    expand_weight,
    contract_weight,
    project_bias,
    output_bias,
    expand_bias,
    contract_bias,
    first_gain,
    first_shift,
    second_gain,
    second_shift,
):
    wide_project, wide_output, wide_expand, wide_contract = (
        lax.all_gather(project_weight, "fsdp", axis=1, tiled=True),
        lax.all_gather(output_weight, "fsdp", axis=1, tiled=True),
        lax.all_gather(expand_weight, "fsdp", axis=1, tiled=True),
        lax.all_gather(contract_weight, "fsdp", axis=1, tiled=True),
    )
    return (
        lax.all_gather(wide_project, "dp", axis=0, tiled=True),
        lax.all_gather(wide_output, "dp", axis=0, tiled=True),
        lax.all_gather(wide_expand, "dp", axis=0, tiled=True),
        lax.all_gather(wide_contract, "dp", axis=0, tiled=True),
        lax.all_gather(project_bias, "dp", axis=0, tiled=True),
        lax.all_gather(output_bias, "dp", axis=0, tiled=True),
        lax.all_gather(expand_bias, "dp", axis=0, tiled=True),
        lax.all_gather(contract_bias, "dp", axis=0, tiled=True),
        lax.all_gather(first_gain, "dp", axis=0, tiled=True),
        lax.all_gather(first_shift, "dp", axis=0, tiled=True),
        lax.all_gather(second_gain, "dp", axis=0, tiled=True),
        lax.all_gather(second_shift, "dp", axis=0, tiled=True),
    )


def fetch_backward(
    project_weight,
    output_weight,
    expand_weight,
    contract_weight,
    project_bias,
    output_bias,
    expand_bias,
    contract_bias,
    first_gain,
    first_shift,
    second_gain,
    second_shift,
):
    wide_project, wide_output, wide_expand, wide_contract = (
        lax.all_gather(project_weight, "fsdp", axis=1, tiled=True),
        lax.all_gather(output_weight, "fsdp", axis=1, tiled=True),
        lax.all_gather(expand_weight, "fsdp", axis=1, tiled=True),
        lax.all_gather(contract_weight, "fsdp", axis=1, tiled=True),
    )
    return (
        lax.all_gather(wide_project, "dp", axis=0, tiled=True),
        lax.all_gather(wide_output, "dp", axis=0, tiled=True),
        lax.all_gather(wide_expand, "dp", axis=0, tiled=True),
        lax.all_gather(wide_contract, "dp", axis=0, tiled=True),
        lax.all_gather(project_bias, "dp", axis=0, tiled=True),
        lax.all_gather(output_bias, "dp", axis=0, tiled=True),
        lax.all_gather(expand_bias, "dp", axis=0, tiled=True),
        lax.all_gather(contract_bias, "dp", axis=0, tiled=True),
        lax.all_gather(first_gain, "dp", axis=0, tiled=True),
        lax.all_gather(first_shift, "dp", axis=0, tiled=True),
        lax.all_gather(second_gain, "dp", axis=0, tiled=True),
        lax.all_gather(second_shift, "dp", axis=0, tiled=True),
    )


def split_heads(cell_rows, block_rows):
    slot_count = cell_rows.shape[0]
    width = cell_rows.shape[1] // 3
    query_blocks = cell_rows[:, :width].reshape(slot_count // block_rows, block_rows, H, HD)
    keys_all = cell_rows[:, width : 2 * width].reshape(slot_count, H, HD)
    values_all = cell_rows[:, 2 * width :].reshape(slot_count, H, HD)
    return (query_blocks, keys_all, values_all)


def block_scores(query_block, keys_all, key_live):
    scores = jnp.einsum(
        "qhe,khe->hqk", query_block, keys_all, preferred_element_type=jnp.float32
    ) * HD ** (-0.5)
    return jnp.where(key_live[None, None, :], scores, neg_fill)


def attend_forward(query_block, keys_all, values_all, key_live):
    scores = block_scores(query_block, keys_all, key_live)
    row_max = jnp.max(scores, axis=-1, keepdims=True)
    powers = jnp.exp(scores - row_max)
    row_total = jnp.sum(powers, axis=-1, keepdims=True)
    weights = (powers / row_total).astype(jnp.bfloat16)
    mixed_block = jnp.einsum(
        "hqk,khe->qhe", weights, values_all, preferred_element_type=jnp.float32
    )
    return (mixed_block, (row_max + jnp.log(row_total))[:, :, 0])


def attend_backward(query_block, grad_block, log_block, keys_all, values_all, key_live):
    scores = block_scores(query_block, keys_all, key_live)
    weights = jnp.exp(scores - log_block[:, :, None])
    grad_weights = jnp.einsum(
        "qhe,khe->hqk", grad_block, values_all, preferred_element_type=jnp.float32
    )
    row_inner = jnp.sum(grad_weights * weights, axis=-1, keepdims=True)
    grad_scores = (weights * (grad_weights - row_inner)).astype(jnp.bfloat16)
    grad_query = jnp.einsum(
        "hqk,khe->qhe", grad_scores, keys_all, preferred_element_type=jnp.float32
    ) * HD ** (-0.5)
    grad_key = jnp.einsum(
        "hqk,qhe->khe", grad_scores, query_block, preferred_element_type=jnp.float32
    ) * HD ** (-0.5)
    grad_value = jnp.einsum(
        "hqk,qhe->khe", weights.astype(jnp.bfloat16), grad_block, preferred_element_type=jnp.float32
    )
    return (grad_query, grad_key, grad_value)


def per_device(
    tokens,
    lengths,
    cotangent,
    project_weight,
    project_bias,
    output_weight,
    output_bias,
    expand_weight,
    expand_bias,
    contract_weight,
    contract_bias,
    first_gain,
    first_shift,
    second_gain,
    second_shift,
):
    fetched = fetch_forward(
        project_weight,
        output_weight,
        expand_weight,
        contract_weight,
        project_bias,
        output_bias,
        expand_bias,
        contract_bias,
        first_gain,
        first_shift,
        second_gain,
        second_shift,
    )
    full_project, full_output, full_expand, full_contract = (
        fetched[0],
        fetched[1],
        fetched[2],
        fetched[3],
    )
    vectors = [item.astype(jnp.float32) for item in fetched[4:]]
    bias_project, bias_output, bias_expand, bias_contract = (
        vectors[0],
        vectors[1],
        vectors[2],
        vectors[3],
    )
    gain_one, shift_one, gain_two, shift_two = (vectors[4], vectors[5], vectors[6], vectors[7])
    cell_count = lengths.shape[0]
    slot_count = tokens.shape[0] // cell_count
    width = tokens.shape[1]
    block_rows = min(512, slot_count)
    positions = jnp.arange(slot_count, dtype=jnp.int32)
    live_keys = positions[None, :] < lengths[:, None]
    live_rows = live_keys.reshape(-1)
    rows_in = tokens.astype(jnp.float32)
    normed_one = layer_norm(rows_in, gain_one, shift_one).astype(jnp.bfloat16)
    bias_full = jnp.concatenate(
        [bias_project[:width], jnp.zeros((width,), jnp.float32), bias_project[width:]]
    )
    projected = (matmul(normed_one, full_project) + bias_full).astype(jnp.bfloat16)
    cell_index = 0
    query_blocks, keys_all, values_all = split_heads(projected, block_rows)
    key_live = live_keys[cell_index]
    mixed_blocks, log_blocks = lax.map(
        lambda query_block: attend_forward(query_block, keys_all, values_all, key_live),
        query_blocks,
    )
    mixed_list = mixed_blocks.reshape(slot_count, width)
    log_list = [log_blocks]
    mixed_low = mixed_list.astype(jnp.bfloat16)
    middle = rows_in + (matmul(mixed_low, full_output) + bias_output)
    normed_two = layer_norm(middle, gain_two, shift_two).astype(jnp.bfloat16)
    hidden = matmul(normed_two, full_expand) + bias_expand
    active = gelu_exact(hidden).astype(jnp.bfloat16)
    result = middle + (matmul(active, full_contract) + bias_contract)
    block_out = jnp.where(live_rows[:, None], result, 0.0).astype(jnp.bfloat16)
    again = fetch_backward(
        project_weight,
        output_weight,
        expand_weight,
        contract_weight,
        project_bias,
        output_bias,
        expand_bias,
        contract_bias,
        first_gain,
        first_shift,
        second_gain,
        second_shift,
    )
    back_project, back_output, back_expand, back_contract = (again[0], again[1], again[2], again[3])
    grad_out = jnp.where(live_rows[:, None], cotangent.astype(jnp.float32), 0.0)
    grad_out_low = grad_out.astype(jnp.bfloat16)
    grad_contract = over_rows(active, grad_out_low)
    grad_contract_bias = jnp.sum(grad_out, axis=0)
    grad_active = over_columns(grad_out_low, back_contract)
    gelu_value, gelu_pull = jax.vjp(gelu_exact, hidden)
    grad_hidden = gelu_pull(grad_active)[0].astype(jnp.bfloat16)
    grad_expand = over_rows(normed_two, grad_hidden)
    grad_expand_bias = jnp.sum(grad_hidden.astype(jnp.float32), axis=0)
    grad_normed_two = over_columns(grad_hidden, back_expand)
    norm_value, second_pull = jax.vjp(layer_norm, middle, gain_two, shift_two)
    grad_middle, grad_gain_two, grad_shift_two = second_pull(grad_normed_two)
    grad_middle = grad_middle + grad_out
    grad_branch = grad_middle.astype(jnp.bfloat16)
    grad_output = over_rows(mixed_low, grad_branch)
    grad_output_bias = jnp.sum(grad_branch.astype(jnp.float32), axis=0)
    grad_mixed = over_columns(grad_branch, back_output).astype(jnp.bfloat16)
    cell_index = 0
    query_blocks, keys_all, values_all = split_heads(projected, block_rows)
    key_live = live_keys[cell_index]
    grad_blocks = grad_mixed.reshape(slot_count // block_rows, block_rows, H, HD)

    def visit_block(carried, inputs):
        query_block, grad_block, log_block = inputs
        grad_query, grad_key, grad_value = attend_backward(
            query_block, grad_block, log_block, keys_all, values_all, key_live
        )
        return ((carried[0] + grad_key, carried[1] + grad_value), grad_query)

    initial = (
        jnp.zeros((slot_count, H, HD), jnp.float32),
        jnp.zeros((slot_count, H, HD), jnp.float32),
    )
    (key_sums, value_sums), query_grads = lax.scan(
        visit_block, initial, (query_blocks, grad_blocks, log_list[cell_index])
    )
    grad_cells = jnp.concatenate(
        [
            query_grads.reshape(slot_count, width),
            key_sums.reshape(slot_count, width),
            value_sums.reshape(slot_count, width),
        ],
        axis=1,
    )
    grad_projected = grad_cells.astype(jnp.bfloat16)
    grad_project = over_rows(normed_one, grad_projected)
    column_sums = jnp.sum(grad_projected.astype(jnp.float32), axis=0)
    grad_project_bias = jnp.concatenate([column_sums[:width], column_sums[2 * width :]])
    grad_normed_one = over_columns(grad_projected, back_project)
    first_value, first_pull = jax.vjp(layer_norm, rows_in, gain_one, shift_one)
    grad_rows_in, grad_gain_one, grad_shift_one = first_pull(grad_normed_one)
    tokens_grad = (grad_rows_in + grad_middle).astype(jnp.bfloat16)
    reduced = (
        lax.psum_scatter(grad_project, "dp", scatter_dimension=0, tiled=True),
        lax.psum_scatter(grad_output, "dp", scatter_dimension=0, tiled=True),
        lax.psum_scatter(grad_expand, "dp", scatter_dimension=0, tiled=True),
        lax.psum_scatter(grad_contract, "dp", scatter_dimension=0, tiled=True),
        lax.psum_scatter(grad_project_bias, "dp", scatter_dimension=0, tiled=True),
        lax.psum_scatter(grad_output_bias, "dp", scatter_dimension=0, tiled=True),
        lax.psum_scatter(grad_expand_bias, "dp", scatter_dimension=0, tiled=True),
        lax.psum_scatter(grad_contract_bias, "dp", scatter_dimension=0, tiled=True),
        lax.psum_scatter(grad_gain_one, "dp", scatter_dimension=0, tiled=True),
        lax.psum_scatter(grad_shift_one, "dp", scatter_dimension=0, tiled=True),
        lax.psum_scatter(grad_gain_two, "dp", scatter_dimension=0, tiled=True),
        lax.psum_scatter(grad_shift_two, "dp", scatter_dimension=0, tiled=True),
    )
    shard_project, shard_output, shard_expand, shard_contract = (
        lax.psum_scatter(
            reduced[0].astype(jnp.bfloat16), "fsdp", scatter_dimension=1, tiled=True
        ).astype(jnp.float32),
        lax.psum_scatter(
            reduced[1].astype(jnp.bfloat16), "fsdp", scatter_dimension=1, tiled=True
        ).astype(jnp.float32),
        lax.psum_scatter(
            reduced[2].astype(jnp.bfloat16), "fsdp", scatter_dimension=1, tiled=True
        ).astype(jnp.float32),
        lax.psum_scatter(
            reduced[3].astype(jnp.bfloat16), "fsdp", scatter_dimension=1, tiled=True
        ).astype(jnp.float32),
    )
    summed = lax.psum(
        (
            reduced[4],
            reduced[5],
            reduced[6],
            reduced[7],
            reduced[8],
            reduced[9],
            reduced[10],
            reduced[11],
        ),
        "fsdp",
    )
    return (
        block_out,
        tokens_grad,
        shard_project,
        summed[0],
        shard_output,
        summed[1],
        shard_expand,
        summed[2],
        shard_contract,
        summed[3],
        summed[4],
        summed[5],
        summed[6],
        summed[7],
    )


def scatter_events(link, place, col, pair_of, lc, lxh, lyh, lx, ly):
    p = place
    family = (p.dc, p.dx + p.dc - p.d, p.dy + p.dc - p.d, p.dd + p.dc - p.d)
    cs = [link.slot() for _ in range(4)]
    hx, hy, fx, fy = (link.slot() for _ in range(4))
    got = link.got

    def add(target, *terms):
        flat = len(target.shape) == 2

        def body(i, _):
            at = (pl.ds(mo(i * 16, 16), 16), slice(None)) if flat else (i,)
            total = target[at].astype(F32)
            for term in terms:
                total = total + term[at].astype(F32)
            target[at] = total.astype(BF)
            return 0

        lax.fori_loop(0, target.shape[0] // 16 if flat else target.shape[0], body, 0)

    def to_sibling(which):
        link.send(cs[which], col(family[which]), lc.at[which], "c", lambda: col(0))

    def halves():
        got(cs[3], lc.at[3])
        add(col(p.dd), lc.at[3])
        link.send(hx, pair_of(col(p.dd), 0), lxh, "x", lambda: lxh)
        link.send(hy, pair_of(col(p.dd), 1), lyh, "y", lambda: lyh)

    def near():
        got(cs[1], lc.at[1])
        got(cs[2], lc.at[2])
        add(col(p.dx), lc.at[1])
        add(col(p.dy), lc.at[2])

    def pass_y():
        got(hx, lxh)
        add(pair_of(col(p.dy), 0), lxh)
        link.send(fy, col(p.dy), ly, "y", lambda: ly)

    def pass_x():
        got(hy, lyh)
        add(pair_of(col(p.dx), 1), lyh)
        link.send(fx, col(p.dx), lx, "x", lambda: lx)

    def own():
        got(cs[0], lc.at[0])

    def total():
        got(fx, lx)
        got(fy, ly)
        add(col(p.d), lc.at[0], lx, ly)

    return to_sibling, [halves, near, pass_y, pass_x, own, total]


def z_sum(link, place, block, lz, finish):
    p = place
    zs = link.slot(4)

    def send():
        for step in (1, 3, 2):
            link.send(zs + step, block(p.zt(step)), lz.at[step], step, lambda: lz.at[0])

    def last():
        total = block(p.z)[...].astype(F32)
        for step in (1, 3, 2):
            link.got(zs + step, lz.at[step])
            total = total + lz[step].astype(F32)
        finish(total)

    return send, last


def gelu_pair(value):
    lift = 0.5 * (1.0 + lax.erf(value * 0.7071067811865476))
    bell = jnp.exp(value * value * -0.5) * 0.3989422804014327
    return value * lift, lift + value * bell


def second_kernel(length_ref, x_hbm, cot_hbm, mixed_hbm, wo_hbm, we_hbm, c_hbm, v_ref,
                  block_out, dmixed_out, dmiddle_out, ge_out, go_out, gc_out, vg_out,
                  x_ref, cot_ref, mixed_ref, wo_ref, we, wct, act, slope, middle, n2t, dot_t, mixed_t, dbranch, dout, gc, go, dmixed, bout, vg,
                  lc, lxh, lyh, lx, ly, send_sem, recv_sem, out_sem):
    p = Place()
    T, D = x_ref.shape
    FF = we.shape[1]
    R = D // 8
    Q = FF // 4
    C8 = FF // 8
    link = Link(p, send_sem, recv_sem)
    bc = lambda z, d: wct.at[pl.ds(mo(z * (D // 4), 16), D // 4), pl.ds(mo(d * C8, 128), C8)]
    gather = Gather(link, p, bc)

    to_sibling, scatter = scatter_events(
        link, p, lambda d: gc.at[d], lambda ref, h: ref.at[pl.ds(2 * h, 2)], lc, lxh, lyh, lx, ly)
    load = pltpu.make_async_copy(we_hbm, we, out_sem.at[0])
    columns = [pltpu.make_async_copy(c_hbm.at[z], bc(z, p.d), out_sem.at[19 + z]) for z in range(4)]
    for made in columns:
        made.start()
    halves = [pl.ds(i * (T // 2), T // 2) for i in range(2)]
    early = [[pltpu.make_async_copy(wo_hbm, wo_ref, out_sem.at[12])], []]
    for i, r in enumerate(halves):
        for at, (a, b) in enumerate(((mixed_hbm, mixed_ref), (x_hbm, x_ref), (cot_hbm, cot_ref))):
            early[i].append(pltpu.make_async_copy(a.at[r], b.at[r], out_sem.at[13 + 3 * i + at]))
    for made in early[0] + early[1]:
        made.start()
    load.start()
    enter(p)
    for made in columns:
        made.wait()
    run(*gather.x)()
    for made in early[0] + early[1]:
        made.wait()
    length = length_ref[0]
    LR = 256
    rows = lambda i: pl.ds(mo(i * LR, LR), LR)
    vec = lambda i: v_ref[i:i + 1, 0:D]
    vg[...] = jnp.zeros_like(vg)

    def at(i, spots):
        for where, event in spots:
            pl.when(i == where)(event)

    def norm(value):
        u = value - jnp.mean(value, axis=-1, keepdims=True)
        r = lax.rsqrt(jnp.mean(u * u, axis=-1, keepdims=True) + eps_norm)
        return u * r, r

    def middle_body(i, _):
        r = rows(i)
        value = x_ref[r, :].astype(F32) + (dot(mixed_ref[r, :], wo_ref[...]) + vec(2))
        middle[r, :] = value
        xhat, _ = norm(value)
        n2 = (xhat * vec(6) + vec(7)).astype(BF)
        dmixed[r, :] = n2
        n2t[:, r] = n2.T
        live = iota((LR, D), 0) + i * LR < length
        grad = jnp.where(live, cot_ref[r, :].astype(F32), 0.0)
        vg[7:8, :] += jnp.sum(grad, axis=0, keepdims=True)
        dout[r, :] = grad.astype(BF)
        dot_t[:, r] = grad.astype(BF).T
        mixed_t[:, r] = mixed_ref[r, :].T
        return 0

    lax.fori_loop(0, T // LR, middle_body, 0)
    load.wait()

    def hidden_body(i, _):
        at(i, [(0, gather.t[0]), (1, gather.t[1]), (2, gather.t[2]), (3, gather.t[3])])
        r = rows(i)
        left = dmixed[r, :]
        for j in range(4):
            cols = slice(j * Q, (j + 1) * Q)
            first, second = gelu_pair(dot(left, we[:, cols]) + v_ref[1:2, cols])
            act[r, cols] = first.astype(BF)
            slope[r, cols] = second.astype(BF)
        return 0

    lax.fori_loop(0, T // LR, hidden_body, 0)

    def column(d):
        value = dot(dot_t[...], act[:, pl.ds(mo(d * C8, 128), C8)])
        gc[d] = value.reshape(4, D // 4, C8).astype(BF)

    sib = p.dc - p.d
    turns = (p.dd + sib, p.dd, p.dx + sib, p.dy + sib, p.dx, p.dy, p.d + sib, p.d)

    def column_body(i, _):
        d = turns[7]
        for k in range(7):
            d = jnp.where(i == k, turns[k], d)
        column(d)
        at(i, [(0, lambda: to_sibling(3)), (2, lambda: to_sibling(1)), (3, run(lambda: to_sibling(2), gather.q[0])),
               (5, run(gather.q[1], gather.q[2], scatter[0])), (6, lambda: to_sibling(0))])
        return 0

    lax.fori_loop(0, 8, column_body, 0)
    run(gather.q[3], scatter[1], gather.close)()

    def back_body(i, _):
        at(i, [(1, run(scatter[2], scatter[3], scatter[4]))])
        r = rows(i)
        grad_low = dout[r, :]
        result = middle[r, :] + vec(3)
        for j in range(4):
            cols = slice(j * Q, (j + 1) * Q)
            dh = dot(grad_low, wct[:, cols]) * slope[r, cols].astype(F32)
            low = dh.astype(BF)
            slope[r, cols] = low
            vg[3 + j:4 + j, :] += jnp.sum(low.astype(F32), axis=0, keepdims=True)
        result = result + dot_nt(act[r, :], wct[...])
        dn = dot_nt(slope[r, :], we[...])
        live = iota((LR, D), 0) + i * LR < length
        bout[r, :] = jnp.where(live, result, 0.0).astype(BF)
        xhat, spread = norm(middle[r, :])
        vg[10:11, :] += jnp.sum(dn * xhat, axis=0, keepdims=True)
        vg[11:12, :] += jnp.sum(dn, axis=0, keepdims=True)
        gx = dn * vec(6)
        back = spread * (gx - jnp.mean(gx, axis=-1, keepdims=True)
                         - xhat * jnp.mean(gx * xhat, axis=-1, keepdims=True))
        total = dout[r, :].astype(F32) + back
        middle[r, :] = total
        branch = total.astype(BF)
        dbranch[r, :] = branch
        vg[2:3, :] += jnp.sum(branch.astype(F32), axis=0, keepdims=True)
        dmixed[r, :] = dot_nt(branch, wo_ref[...]).astype(BF)
        return 0

    lax.fori_loop(0, T // LR, back_body, 0)
    outs = []

    def out(source, target):
        made = pltpu.make_async_copy(source, target, out_sem.at[1 + len(outs)])
        made.start()
        outs.append(made)

    out(bout, block_out)
    out(dmixed, dmixed_out)
    out(middle, dmiddle_out)
    for z in range(4):
        cols = slice(3 * z // 2 * 128, 3 * z // 2 * 128 + 256)
        go[:, z] = dot(mixed_t[...], dbranch[:, cols]).reshape(8, R, 256).astype(BF)
    out(go, go_out)
    for z in range(4):
        act[0:D, z * Q:(z + 1) * Q] = dot(n2t[...], slope[:, z * Q:(z + 1) * Q]).astype(BF)
        out(act.at[0:D, z * Q:(z + 1) * Q], ge_out.at[:, z * Q:(z + 1) * Q])
        if z == 2:
            scatter[5]()
            out(gc.at[p.d], gc_out)
    vg_out[...] = vg[...]
    link.finish()
    for made in outs:
        made.wait()


ANY = pl.BlockSpec(memory_space=pl.ANY)
VM = pl.BlockSpec(memory_space=pltpu.VMEM)
SM = pl.BlockSpec(memory_space=pltpu.SMEM)
sds = jax.ShapeDtypeStruct


def second_call(length, x, cot, mixed, wo, we, wc, v):
    T, D = x.shape
    FF = we.shape[1]
    n = 36 + 8
    R, C8, Z = D // 8, FF // 8, D // 4
    vm = pltpu.VMEM
    return pl.pallas_call(
        second_kernel,
        in_specs=[SM] + [ANY] * 6 + [VM],
        out_specs=[ANY] * 6 + [VM],
        out_shape=[sds((T, D), BF), sds((T, D), BF), sds((T, D), F32), sds((D, FF), BF), sds((8, 4, R, 256), BF),
                   sds((4, Z, C8), BF), sds((16, D), F32)],
        scratch_shapes=[
            vm((T, D), BF), vm((T, D), BF), vm((T, D), BF), vm((D, D), BF), vm((D, FF), BF), vm((D, FF), BF), vm((T, FF), BF), vm((T, FF), BF), vm((T, D), F32),
            vm((D, T), BF), vm((D, T), BF), vm((D, T), BF), vm((T, D), BF), vm((T, D), BF),
            vm((8, 4, Z, C8), BF), vm((8, 4, R, 256), BF), vm((T, D), BF), vm((T, D), BF), vm((16, D), F32),
            vm((4, 4, Z, C8), BF), vm((2, Z, C8), BF), vm((2, Z, C8), BF), vm((4, Z, C8), BF), vm((4, Z, C8), BF),
            pltpu.SemaphoreType.DMA((n,)), pltpu.SemaphoreType.DMA((n,)), pltpu.SemaphoreType.DMA((23,)),
        ],
        compiler_params=pltpu.CompilerParams(
            collective_id=1, has_side_effects=True, vmem_limit_bytes=62 << 20),
        name="second_part",
    )(length, x, cot, mixed, wo, we, wc, v)


def third_kernel(length_ref, proj_hbm, qa_hbm, mixed_hbm, dm_hbm, n1_hbm, wp_hbm, x_hbm, dmiddle_hbm, ge_hbm, go_hbm,
                 gc_hbm, vg_ref, v_ref,
                 tokens_out, gp_out, go_out, ge_out, gc_out, vec_out,
                 proj, qa, mixed, dm, n1, n1t, wpp, x, dmiddle, ge, go, dproj, tg, gp,
                 ka, da, dq, va, kt, vs, vo, vl, vz,
                 lce, lxhe, lyhe, lxe, lye, lze, lco, lxho, lyho, lxo, lyo, lzo,
                 lcp, lxhp, lyhp, lxp, lyp, lzp, gpw, gcol, lzc,
                 send_sem, recv_sem, load_sem):
    p = Place()
    T, D = x.shape
    FF = ge.shape[1]
    R = D // 8
    Q = FF // 4
    pairs = H // 2
    KB = 256
    parts = 2
    link = Link(p, send_sem, recv_sem)
    loads = []

    def load(source, target):
        made = pltpu.make_async_copy(source, target, load_sem.at[len(loads)])
        made.start()
        loads.append(made)
        return made

    first_loads = [load(a, b) for a, b in ((proj_hbm, proj), (qa_hbm, qa), (mixed_hbm, mixed), (dm_hbm, dm))]
    ge_load, gc_load, go_load, n1_load = load(ge_hbm, ge), load(gc_hbm, gcol), load(go_hbm, go), load(n1_hbm, n1)
    late = [load(x_hbm, x), load(dmiddle_hbm, dmiddle)]
    for i in range(pairs):
        for s in range(3):
            late.append(load(wp_hbm.at[:, pl.ds((s * pairs + i) * 128, 128)],
                             wpp.at[:, pl.ds((i * 3 + s) * 128, 128)]))

    def finish_e(total):
        ge_out[...] = total

    def finish_o(total):
        go_out[...] = jnp.where(p.odd == 0, total[:, 0:192], total[:, 64:256])

    rows_of = lambda d: pl.ds(mo(d * R, 16), R)
    def finish_c(total):
        gc_out[...] = total

    e_col, o_col = (lambda d: ge.at[rows_of(d), :]), (lambda d: go.at[d])
    e_sib, ev_e = scatter_events(
        link, p, e_col, lambda ref, h: ref.at[:, pl.ds(h * (FF // 2), FF // 2)], lce, lxhe, lyhe, lxe, lye)
    o_sib, ev_o = scatter_events(
        link, p, o_col, lambda ref, h: ref.at[pl.ds(2 * h, 2)], lco, lxho, lyho, lxo, lyo)
    e_send, e_last = z_sum(link, p, lambda z: e_col(p.d).at[:, pl.ds(mo(z * Q, 128), Q)], lze, finish_e)
    o_send, o_last = z_sum(link, p, lambda z: o_col(p.d).at[z], lzo, finish_o)
    c_send, c_last = z_sum(link, p, lambda z: gcol.at[z], lzc, finish_c)
    ended = []
    combos = []
    for i in range(pairs):
        for s in range(3):
            tile = s * pairs + i
            for owner in range(4):
                left = 9 * owner // 2
                if left <= tile < left + 5:
                    combos.append((i, s, owner, tile - left))
    assert len(combos) == 20
    z_slots = [[link.slot() for _ in range(3)] for _ in combos]

    def pair_scatter(i):
        column = lambda d: gp.at[i, d]
        sib, events = scatter_events(
            link, p, column, lambda ref, h: ref.at[pl.ds(h * (R // 2), R // 2)],
            lcp.at[i], lxhp.at[i], lyhp.at[i], lxp.at[i], lyp.at[i])
        mine = [(at, c) for at, c in enumerate(combos) if c[0] == i]

        def along(add_own):
            def run():
                add_own()
                for at, (_, s, owner, _) in mine:
                    @pl.when(p.z != owner)
                    def _():
                        step = lax.rem(owner - p.z + 4, 4)
                        part = column(p.d).at[:, pl.ds(s * 128, 128)]
                        link.copy(z_slots[at][0] + step - 1, part, lzp.at[at, step - 1], ("z", owner)).start()
            return run

        def last():
            for at, (_, s, owner, place) in mine:
                @pl.when(p.z == owner)
                def _():
                    total = gp[i, p.d, :, s * 128:(s + 1) * 128].astype(F32)
                    for step in range(1, 4):
                        link.got(z_slots[at][step - 1], lzp.at[at, step - 1])
                        total = total + lzp[at, step - 1].astype(F32)
                    gpw[:, place * 128:(place + 1) * 128] = total

        def ending():
            for at, (_, s, owner, _) in mine:
                @pl.when(p.z != owner)
                def _():
                    step = lax.rem(owner - p.z + 4, 4)
                    view = lzp.at[at, 0]
                    link.copy(z_slots[at][0] + step - 1, view, view, "x").wait_send()

        ended.append(ending)

        def start():
            for k in (3, 1, 2, 0):
                sib(k)

        return [start] + events[:5] + [along(events[5]), last]

    ev_p = [pair_scatter(i) for i in range(pairs)]

    enter(p, wide=True)
    for made in first_loads:
        made.wait()
    length = length_ref[0]

    def start_e():
        ge_load.wait()
        for k in (3, 1, 2, 0):
            e_sib(k)

    def start_o():
        go_load.wait()
        for k in (3, 1, 2, 0):
            o_sib(k)

    def turn_n1():
        n1_load.wait()
        for i in range(T // 256):
            n1t[:, i * 256:(i + 1) * 256] = n1[i * 256:(i + 1) * 256, :].T

    def start_c():
        gc_load.wait()
        c_send()

    e, o = ev_e, ev_o
    q = ev_p
    timeline = [
        (0, start_c), (0, start_e), (0, start_o), (0, turn_n1), (1, e[0]), (2, e[1]), (2, e[4]), (2, o[0]), (2, o[1]), (2, o[4]),
        (2, q[0][0]), (3, q[0][1]), (3, q[0][2]), (3, q[0][5]), (4, e[2]), (4, e[3]), (4, c_last), (4, o[2]), (4, o[3]),
        (4, q[0][3]), (4, q[0][4]), (4, q[1][0]), (5, q[1][1]), (5, q[1][2]), (5, q[1][5]), (6, q[2][0]),
        (7, q[2][1]), (7, q[2][2]), (7, q[2][5]), (8, e[5]), (8, e_send), (8, q[3][0]), (9, o[5]), (9, o_send),
        (9, q[3][1]), (9, q[3][2]), (9, q[3][5]), (10, q[0][6]), (10, q[1][3]), (10, q[1][4]), (10, q[2][3]), (10, q[2][4]),
        (10, q[3][3]), (10, q[3][4]), (10, q[4][0]), (11, q[4][1]), (11, q[4][2]), (11, q[4][5])]
    timeline.sort(key=lambda e: e[0])

    def body(step, _):
        for at, event in timeline:
            if at < pairs * parts:
                pl.when(step == at)(event)
        pair = lax.div(step, parts)
        part = lax.rem(step, parts)
        ps = lambda off: pl.ds(mo(off + pair * 128, 128), 128)
        own = lambda s: pl.ds(mo(pair * 384 + s * 128, 128), 128)

        @pl.when(part == 0)
        def _():
            lane, row = iota((T, 128), 1), iota((T, 128), 0)
            k = proj[:, ps(D)].astype(F32)
            v = proj[:, ps(2 * D)].astype(F32)
            do = dm[:, ps(0)].astype(F32)
            pr = do * mixed[:, ps(0)].astype(F32)
            dead = jnp.where(row < length, 0.0, neg_fill)
            for head in range(2):
                keep = (lane < 64) if head == 0 else (lane >= 64)
                delta = jnp.sum(jnp.where(keep, pr, 0.0), axis=-1, keepdims=True)
                one, two, three = split3(-delta)
                da[head] = extend(head, do, lane, one, two, three, 0.0)
                ka[head] = extend(head, k, lane, 1.0, 1.0, 1.0, dead)
                va[head] = extend(head, v, lane, 1.0, 1.0, 1.0, 0.0)
                kt[head] = jnp.where(keep, k, 0.0).astype(BF).T
            dq[...] = jnp.zeros_like(dq)

        lk = iota((KB, 128), 1)
        spans = [pl.ds(mo(part * (T // parts) + i * KB, KB), KB) for i in range(T // parts // KB)]
        items = [(head, r) for r in spans for head in range(2)]
        kept = {}

        def products(n):
            head, r = items[n]
            return dot_nt(ka[head, r, :], qa[pair * 2 + head]), dot_nt(va[head, r, :], da[head])

        def weigh(scores, grads):
            weights = jnp.exp(scores)
            return weights.astype(BF), (weights * grads).astype(BF)

        def finish(n, low, ds):
            head, r = items[n]
            kept[n] = dot(ds, qa[pair * 2 + head]), dot(low, da[head])
            dq[head] += dot(kt[head, :, r], ds)
            if head == 1:
                dproj[r, own(1)] = jnp.where(lk < 64, kept[n - 1][0], kept[n][0]).astype(BF)
                dproj[r, own(2)] = jnp.where(lk < 64, kept[n - 1][1], kept[n][1]).astype(BF)

        value, waiting = products(0), None
        for n in range(len(items)):
            following = products(n + 1) if n + 1 < len(items) else None
            done = weigh(*value)
            if waiting is not None:
                finish(n - 1, *waiting)
            value, waiting = following, done
        finish(len(items) - 1, *waiting)

        @pl.when(part == parts - 1)
        def _():
            dproj[:, own(0)] = ((dq[0] + dq[1]) * (HD ** -0.5)).T.astype(BF)
            value = dot(n1t[...], dproj[:, pl.ds(mo(pair * 384, 128), 384)])
            gp[pair] = value.reshape(8, R, 384).astype(BF)

        return 0

    lax.fori_loop(0, pairs * parts, body, 0)
    ev_p[pairs - 1][0]()
    for made in late:
        made.wait()
    vs[...] = vg_ref[...]
    LR = 256

    def norm_body(i, _):
        def spot(where, events):
            @pl.when(i == where)
            def _():
                for event in events:
                    event()

        spot(0, [e_last, q[1][6], q[2][6], q[3][6], q[4][3], q[4][4]])
        spot(1, q[5][1:3] + q[5][5:6])
        spot(2, [o_last, q[0][7], q[1][7], q[4][6], q[2][7]])
        spot(3, q[5][3:5] + q[3][7:8])
        r = pl.ds(mo(i * LR, LR), LR)
        left = dproj[r, :]
        dn = dot_nt(left, wpp[...])
        sums = jnp.sum(left.astype(F32), axis=0, keepdims=True)
        for j in range(pairs):
            vs[0:1, j * 128:(j + 1) * 128] += sums[:, j * 384:j * 384 + 128]
            vs[1:2, j * 128:(j + 1) * 128] += sums[:, j * 384 + 256:j * 384 + 384]
        value = x[r, :].astype(F32)
        u = value - jnp.mean(value, axis=-1, keepdims=True)
        spread = lax.rsqrt(jnp.mean(u * u, axis=-1, keepdims=True) + eps_norm)
        xhat = u * spread
        vs[8:9, :] += jnp.sum(dn * xhat, axis=0, keepdims=True)
        vs[9:10, :] += jnp.sum(dn, axis=0, keepdims=True)
        gx = dn * v_ref[4:5, 0:D]
        back = spread * (gx - jnp.mean(gx, axis=-1, keepdims=True)
                         - xhat * jnp.mean(gx * xhat, axis=-1, keepdims=True))
        tg[r, :] = (back + dmiddle[r, :]).astype(BF)
        return 0

    lax.fori_loop(0, T // LR, norm_body, 0)
    out = load(tg, tokens_out)
    v_slots = link.slot(16)
    for d in range(8):
        line = lambda row, at, n: jnp.concatenate(
            [vs[row:row + 1, at:at + n], jnp.zeros((1, 384 - n), F32)], axis=1) if n < 384 else vs[row:row + 1, at:at + n]
        vo[d] = jnp.concatenate(
            [line(d // 4, d % 4 * 2 * R, 2 * R), line(2, d * R, R), line(3 + d // 2, d % 2 * 4 * R, 4 * R)]
            + [line(row, d * R, R) for row in (7, 8, 9, 10, 11)], axis=0)
    for d in range(8):
        @pl.when(p.d != d)
        def _():
            link.copy(v_slots + d, vo.at[d], vl.at[p.d], ("d", d), land=v_slots + p.d).start()
    for event in (q[4][7], q[5][6]):
        event()
    vl[p.d] = vo[p.d]
    for d in range(8):
        @pl.when(p.d != d)
        def _():
            link.got(v_slots + d, vl.at[d])
    own = vl[0]
    for d in range(1, 8):
        own = own + vl[d]
    vz[p.z] = own
    for k in (1, 2, 3):
        link.send(v_slots + 8 + k, vz.at[p.z], vz.at[p.z], ("z", p.order[k]), lambda: vz.at[0], land=v_slots + 12 + p.z)
    q[5][7]()
    gp_out[...] = jnp.where(p.odd == 0, gpw[:, 0:576], gpw[:, 64:640])
    for k in (1, 2, 3):
        link.got(v_slots + 12 + p.order[k], vz.at[p.order[k]])
    vec_out[...] = vz[0] + vz[1] + vz[2] + vz[3]
    for d in range(8):
        @pl.when(p.d != d)
        def _():
            link.copy(v_slots + d, vo.at[d], vo.at[d], "x").wait_send()
    link.finish()
    for ending in ended:
        ending()
    out.wait()


def third_call(length, proj, qa, mixed, dm, n1, wp, x, dmiddle, ge, go, gc, vg, v):
    T, D = x.shape
    FF = ge.shape[1]
    R, Q, pairs = D // 8, FF // 4, H // 2
    vm = pltpu.VMEM
    n = 8 * 8 + 12 + 60 + 16
    return pl.pallas_call(
        third_kernel,
        in_specs=[SM] + [ANY] * 11 + [VM] * 2,
        out_specs=[ANY] + [VM] * 5,
        out_shape=[sds((T, D), BF), sds((R, 3 * D // 4), F32), sds((R, D // 4), F32), sds((R, Q), F32), sds((D // 4, FF // 8), F32),
                   sds((8, 384), F32)],
        scratch_shapes=[
            vm((T, 3 * D), BF), vm((H, T, 128), BF), vm((T, D), BF), vm((T, D), BF), vm((T, D), BF), vm((D, T), BF),
            vm((D, 3 * D), BF), vm((T, D), BF), vm((T, D), F32), vm((D, FF), BF), vm((8, 4, R, 256), BF),
            vm((T, 3 * D), BF), vm((T, D), BF), vm((pairs, 8, R, 384), BF),
            vm((2, T, 128), BF), vm((2, T, 128), BF), vm((2, 128, T), F32), vm((2, T, 128), BF), vm((2, 128, T), BF),
            vm((16, D), F32), vm((8, 8, 384), F32), vm((8, 8, 384), F32), vm((4, 8, 384), F32),
            vm((4, R, FF), BF), vm((R, FF // 2), BF), vm((R, FF // 2), BF), vm((R, FF), BF), vm((R, FF), BF), vm((4, R, Q), BF),
            vm((4, 4, R, 256), BF), vm((2, R, 256), BF), vm((2, R, 256), BF), vm((4, R, 256), BF), vm((4, R, 256), BF),
            vm((4, R, 256), BF),
            vm((pairs, 4, R, 384), BF), vm((pairs, R // 2, 384), BF), vm((pairs, R // 2, 384), BF),
            vm((pairs, R, 384), BF), vm((pairs, R, 384), BF), vm((20, 3, R, 128), BF), vm((R, 640), F32),
            vm((4, D // 4, FF // 8), BF), vm((4, D // 4, FF // 8), BF),
            pltpu.SemaphoreType.DMA((n,)), pltpu.SemaphoreType.DMA((n,)), pltpu.SemaphoreType.DMA((29,)),
        ],
        compiler_params=pltpu.CompilerParams(
            collective_id=2, has_side_effects=True, vmem_limit_bytes=63 << 20),
        name="third_part",
    )(length, proj, qa, mixed, dm, n1, wp, x, dmiddle, ge, go, gc, vg, v)


def last_kernel(block_in, tokens_in, p_in, o_in, e_in, c_in, vec_in,
                block_out, tokens_out, p_out, o_out, e_out, c_out, *rest):
    vectors, held, vec, sem = rest[:8], rest[8:14], rest[14], rest[15]
    parts = 2
    rows = block_in.shape[0] // parts
    whole = lambda ref: ref
    legs = []
    for i in range(parts):
        part = lambda ref, i=i: ref.at[pl.ds(i * rows, rows)]
        legs += [(part, block_in, held[0], block_out), (part, tokens_in, held[1], tokens_out)]
    legs += [(whole, a, b, c) for a, b, c in zip((p_in, o_in, e_in, c_in), held[2:], (p_out, o_out, e_out, c_out))]
    first = pltpu.make_async_copy(vec_in, vec, sem.at[2 * len(legs)])
    first.start()
    ins = [pltpu.make_async_copy(part(a), part(b), sem.at[k]) for k, (part, a, b, _) in enumerate(legs)]
    outs = [pltpu.make_async_copy(part(b), part(c), sem.at[len(legs) + k]) for k, (part, _, b, c) in enumerate(legs)]
    for made in ins:
        made.start()
    for came, goes in zip(ins, outs):
        came.wait()
        goes.start()
    first.wait()
    for at, target in enumerate(vectors):
        n = target.shape[0]
        target[...] = vec[at:at + 1, 0:n].reshape(n)
    for goes in outs:
        goes.wait()


def last_call(sizes, *arrays):
    return pl.pallas_call(
        last_kernel,
        in_specs=[ANY] * 7,
        out_specs=[ANY] * 6 + [VM] * 8,
        out_shape=[sds(item.shape, item.dtype) for item in arrays[:6]] + [sds((n,), F32) for n in sizes],
        scratch_shapes=[pltpu.VMEM(item.shape, item.dtype) for item in arrays] + [pltpu.SemaphoreType.DMA((17,))],
        compiler_params=pltpu.CompilerParams(vmem_limit_bytes=63 << 20),
        name="last_part",
    )(*arrays)


def per_device_fast(tokens, lengths, cotangent, project_weight, project_bias, output_weight, output_bias,
                    expand_weight, expand_bias, contract_weight, contract_bias, first_gain, first_shift,
                    second_gain, second_shift):
    vectors = (project_bias, output_bias, expand_bias, contract_bias, first_gain, first_shift, second_gain, second_shift)
    normed_one, projected, mixed, qa, full_project, full_output, full_expand, cc, v = first_call(
        lengths, tokens, project_weight, output_weight, expand_weight, contract_weight.T, vectors)
    block_out, grad_mixed, grad_middle, ge, go, gc, vg = second_call(
        lengths, tokens, cotangent, mixed, full_output, full_expand, cc, v)
    third = third_call(
        lengths, projected, qa, mixed, grad_mixed, normed_one, full_project, tokens, grad_middle, ge, go, gc, vg, v)
    out = last_call([item.shape[0] for item in vectors], block_out, *third)
    return (out[0], out[1], out[2], out[6], out[3], out[7], out[4], out[8], out[5].T, *out[9:])


def solution(mesh):
    both, rows, grid = P(("dp", "fsdp"), None), P("dp"), P("dp", "fsdp")
    weights = (grid, rows, grid, rows, grid, rows, grid, rows)
    fast = mesh.shape["dp"] == 8 and mesh.shape["fsdp"] == 4
    return jax.shard_map(
        per_device_fast if fast else per_device,
        mesh=mesh,
        in_specs=(both, P(("dp", "fsdp")), both) + weights + (rows,) * 4,
        out_specs=(both, both) + weights + (rows,) * 4,
        check_vma=False,
    )
```

profile of v0, /device:TPU:0, one launch (start us, length us, event | category | flops | bytes accessed | tf_op | source)
XLA Modules:
  0.0 211.0 jit_solution(15355358041202565021)
XLA Ops:
  1.3 66.0 %first_part.1 = (bf16[1024,768]{1,0:T(8,128)(2,1)}, bf16[1024,2304]{1,0:T(8,128)(2,1)}, bf16[1024,768]{1,0:T(8,128)(2,1)}, bf16[12,1024,128]{2,1,0:T(8,128)(2,1)...) custom-call(s32[1]{0:T(128)S(6)} %copy.29.length_ref, ...), custom_call_target="tpu_custom_call" | custom-call | tf_op jit(solution)/shard_map/first_part/pallas_call | solution.py:444
  67.3 59.7 %second_part.1 = (bf16[1024,768]{1,0:T(8,128)(2,1)}, bf16[1024,768]{1,0:T(8,128)(2,1)}, f32[1024,768]{1,0:T(8,128)}, bf16[768,3072]{1,0:T(8,128)(2,1)}, bf16[8,4...) custom-call(s32[1]{0:T(128)S(6)} %copy.29.length_ref, bf16[1024,768]{1,0:T(8,128)(2,1)} %x_hbm.3, ...), custom_call_target="tpu_custom_call" | custom-call | tf_op jit(solution)/shard_map/second_part/pallas_call | solution.py:1059
  127.0 80.0 %third_part.1 = (bf16[1024,768]{1,0:T(8,128)(2,1)}, f32[96,576]{1,0:T(8,128)}, f32[96,192]{1,0:T(8,128)}, f32[96,768]{1,0:T(8,128)}, f32[192,384]{1,0:T(8,128)}, /*index=5*/f32[8,384]{1,0:T(8,128)}) custom-call(s32[1]{0:T(128)S(6)} %copy.29.length_ref, bf16[1024,2304]{1,0:T(8,128)(2,1)} %get-tuple-element.56.proj_hbm, ...), custom_call_target="tpu_custom_call" | custom-call | tf_op jit(solution)/shard_map/third_part/pallas_call | solution.py:1371
  207.0 3.8 %last_part.1 = (bf16[1024,768]{1,0:T(8,128)(2,1)}, bf16[1024,768]{1,0:T(8,128)(2,1)}, f32[96,576]{1,0:T(8,128)}, f32[96,192]{1,0:T(8,128)}, f32[96,768]{1,0:T(8,...) custom-call(bf16[1024,768]{1,0:T(8,128)(2,1)} %get-tuple-element.55., ...), custom_call_target="tpu_custom_call" | custom-call | tf_op jit(solution)/shard_map/last_part/pallas_call | solution.py:1426
where the time goes:
time: 211 us
  Pallas kernels  210 us (100%)
    pallas_call x1, Pallas kernels, third_call(): pl.pallas_call(third_kernel, in_specs=[SM] + [ANY] * 11 + [VM] * 2, out_s...  80 us
    pallas_call x1, Pallas kernels, first_call(): pl.pallas_call(first_kernel, in_specs=[S] + [V] * 13, out_specs=[ANY] * 9...  66 us
    pallas_call x1, Pallas kernels, second_call(): pl.pallas_call(second_kernel, in_specs=[SM] + [ANY] * 6 + [VM], out_specs...  59.7 us

commit v1 on v0

--- a/solution.py
+++ b/solution.py
@@ -915,13 +915,13 @@
             early[i].append(pltpu.make_async_copy(a.at[r], b.at[r], out_sem.at[13 + 3 * i + at]))
     for made in early[0] + early[1]:
         made.start()
-    load.start()
     enter(p)
     for made in columns:
         made.wait()
     run(*gather.x)()
     for made in early[0] + early[1]:
         made.wait()
+    load.start()
     length = length_ref[0]
     LR = 256
     rows = lambda i: pl.ds(mo(i * LR, LR), LR)
@@ -1094,19 +1094,20 @@
     link = Link(p, send_sem, recv_sem)
     loads = []
 
-    def load(source, target):
+    def load(source, target, now=True):
         made = pltpu.make_async_copy(source, target, load_sem.at[len(loads)])
-        made.start()
+        if now:
+            made.start()
         loads.append(made)
         return made
 
     first_loads = [load(a, b) for a, b in ((proj_hbm, proj), (qa_hbm, qa), (mixed_hbm, mixed), (dm_hbm, dm))]
-    ge_load, gc_load, go_load, n1_load = load(ge_hbm, ge), load(gc_hbm, gcol), load(go_hbm, go), load(n1_hbm, n1)
-    late = [load(x_hbm, x), load(dmiddle_hbm, dmiddle)]
+    ge_load, gc_load, go_load, n1_load = load(ge_hbm, ge), load(gc_hbm, gcol), load(go_hbm, go), load(n1_hbm, n1, False)
+    late = [load(x_hbm, x, False), load(dmiddle_hbm, dmiddle, False)]
     for i in range(pairs):
         for s in range(3):
             late.append(load(wp_hbm.at[:, pl.ds((s * pairs + i) * 128, 128)],
-                             wpp.at[:, pl.ds((i * 3 + s) * 128, 128)]))
+                             wpp.at[:, pl.ds((i * 3 + s) * 128, 128)], False))
 
     def finish_e(total):
         ge_out[...] = total
@@ -1187,6 +1188,7 @@
     enter(p, wide=True)
     for made in first_loads:
         made.wait()
+    n1_load.start()
     length = length_ref[0]
 
     def start_e():
@@ -1199,6 +1201,10 @@
         for k in (3, 1, 2, 0):
             o_sib(k)
 
+    def start_late():
+        for made in late:
+            made.start()
+
     def turn_n1():
         n1_load.wait()
         for i in range(T // 256):
@@ -1211,7 +1217,7 @@
     e, o = ev_e, ev_o
     q = ev_p
     timeline = [
-        (0, start_c), (0, start_e), (0, start_o), (0, turn_n1), (1, e[0]), (2, e[1]), (2, e[4]), (2, o[0]), (2, o[1]), (2, o[4]),
+        (0, start_c), (0, start_e), (0, start_o), (1, turn_n1), (1, e[0]), (2, start_late), (2, e[1]), (2, e[4]), (2, o[0]), (2, o[1]), (2, o[4]),
         (2, q[0][0]), (3, q[0][1]), (3, q[0][2]), (3, q[0][5]), (4, e[2]), (4, e[3]), (4, c_last), (4, o[2]), (4, o[3]),
         (4, q[0][3]), (4, q[0][4]), (4, q[1][0]), (5, q[1][1]), (5, q[1][2]), (5, q[1][5]), (6, q[2][0]),
         (7, q[2][1]), (7, q[2][2]), (7, q[2][5]), (8, e[5]), (8, e_send), (8, q[3][0]), (9, o[5]), (9, o_send),

time: 211 us -> 211 us (level)
  no operation moved by 1% of the time
where the time goes in v1:
time: 211 us
  Pallas kernels  209 us (99%)
    pallas_call x1, Pallas kernels, third_call(): pl.pallas_call(third_kernel, in_specs=[SM] + [ANY] * 11 + [VM] * 2, out_s...  79.5 us
    pallas_call x1, Pallas kernels, first_call(): pl.pallas_call(first_kernel, in_specs=[S] + [V] * 13, out_specs=[ANY] * 9...  66 us
    pallas_call x1, Pallas kernels, second_call(): pl.pallas_call(second_kernel, in_specs=[SM] + [ANY] * 6 + [VM], out_specs...  59.7 us

profile of v1, /device:TPU:0, one launch (start us, length us, event | category | flops | bytes accessed | tf_op | source)
XLA Modules:
  0.0 210.5 jit_solution(17833941928945879071)
XLA Ops:
  1.3 66.0 %first_part.1 = (bf16[1024,768]{1,0:T(8,128)(2,1)}, bf16[1024,2304]{1,0:T(8,128)(2,1)}, bf16[1024,768]{1,0:T(8,128)(2,1)}, bf16[12,1024,128]{2,1,0:T(8,128)(2,1)...) custom-call(s32[1]{0:T(128)S(6)} %copy.29.length_ref, ...), custom_call_target="tpu_custom_call" | custom-call | tf_op jit(solution)/shard_map/first_part/pallas_call | solution.py:444
  67.3 59.7 %second_part.1 = (bf16[1024,768]{1,0:T(8,128)(2,1)}, bf16[1024,768]{1,0:T(8,128)(2,1)}, f32[1024,768]{1,0:T(8,128)}, bf16[768,3072]{1,0:T(8,128)(2,1)}, bf16[8,4...) custom-call(s32[1]{0:T(128)S(6)} %copy.29.length_ref, bf16[1024,768]{1,0:T(8,128)(2,1)} %x_hbm.3, ...), custom_call_target="tpu_custom_call" | custom-call | tf_op jit(solution)/shard_map/second_part/pallas_call | solution.py:1059
  127.0 79.5 %third_part.1 = (bf16[1024,768]{1,0:T(8,128)(2,1)}, f32[96,576]{1,0:T(8,128)}, f32[96,192]{1,0:T(8,128)}, f32[96,768]{1,0:T(8,128)}, f32[192,384]{1,0:T(8,128)}, /*index=5*/f32[8,384]{1,0:T(8,128)}) custom-call(s32[1]{0:T(128)S(6)} %copy.29.length_ref, bf16[1024,2304]{1,0:T(8,128)(2,1)} %get-tuple-element.56.proj_hbm, ...), custom_call_target="tpu_custom_call" | custom-call | tf_op jit(solution)/shard_map/third_part/pallas_call | solution.py:1377
  206.5 3.8 %last_part.1 = (bf16[1024,768]{1,0:T(8,128)(2,1)}, bf16[1024,768]{1,0:T(8,128)(2,1)}, f32[96,576]{1,0:T(8,128)}, f32[96,192]{1,0:T(8,128)}, f32[96,768]{1,0:T(8,...) custom-call(bf16[1024,768]{1,0:T(8,128)(2,1)} %get-tuple-element.55., ...), custom_call_target="tpu_custom_call" | custom-call | tf_op jit(solution)/shard_map/last_part/pallas_call | solution.py:1432

commit v2 on v1

--- a/solution.py
+++ b/solution.py
@@ -252,9 +252,9 @@
     first_body(length_ref, x_ref, wp_ref, wo_ref, we_ref, wc_ref, vec_refs, *refs)
 
 
-def first_body(length_ref, x_ref, wp_ref, wo_ref, we_ref, wc_ref, vec_refs,
+def first_body(length_ref, x_hbm, wp_ref, wo_ref, we_ref, wc_ref, vec_refs,
                  n1_out, proj_out, mixed_out, qa_out, wp_out, wo_out, we_out, c_out, v_out,
-                 wp_blk, wo_blk, we, wp, wo, vb, n1, proj, mixed, qa, ka, va, vrow, cc,
+                 wp_blk, wo_blk, we, wp, wo, vb, n1, proj, mixed, qa, ka, va, vrow, cc, x_ref,
                  send_sem, recv_sem, out_sem, pair_sem):
     p = Place()
     T, D = x_ref.shape
@@ -274,6 +274,8 @@
     wp_blk[p.z, rows_of(p.d), :] = window(wp_ref[...], p.odd, wp_blk.shape[2])
     wo_blk[p.z, rows_of(p.d), :] = window(wo_ref[...], p.odd, wo_blk.shape[2])
     we[rows_of(p.d), pl.ds(mo(p.z * (FF // 4), 128), FF // 4)] = we_ref[...]
+    x_load = pltpu.make_async_copy(x_hbm, x_ref, out_sem.at[9])
+    x_load.start()
     cc[p.z] = wc_ref[...]
     for i, ref in enumerate(vec_refs):
         vb[p.d, i:i + 1, 0:ref.shape[0]] = ref[...].astype(F32).reshape(1, ref.shape[0]).astype(BF)
@@ -326,6 +328,7 @@
 
     norm_part = lambda k: lax.fori_loop(k * (T // LR // 4), (k + 1) * (T // LR // 4), norm_body, 0)
     g0.t[2]()
+    x_load.wait()
     norm_part(0)
     run(g1.z[2], g1.x[2], g0.q[1])()
     norm_part(1)
@@ -443,7 +446,7 @@
     n = 4 * 36 + 7 + 7
     return pl.pallas_call(
         first_kernel,
-        in_specs=[S] + [V] * 13,
+        in_specs=[S, ANY] + [V] * 12,
         out_specs=[ANY] * 9,
         out_shape=[sds((T, D), BF), sds((T, 3 * D), BF), sds((T, D), BF), sds((H, T, 128), BF),
                    sds((D, 3 * D), BF), sds((D, D), BF), sds((D, FF), BF), sds((4,) + wc.shape, BF), sds((8, FF), F32)],
@@ -453,7 +456,8 @@
             pltpu.VMEM((T, D), BF), pltpu.VMEM((T, 3 * D), BF), pltpu.VMEM((T, D), BF),
             pltpu.VMEM((H, T, 128), BF), pltpu.VMEM((2, T, 128), BF), pltpu.VMEM((2, T, 128), BF),
             pltpu.VMEM((8, FF), F32), pltpu.VMEM((4,) + wc.shape, BF),
-            pltpu.SemaphoreType.DMA((n,)), pltpu.SemaphoreType.DMA((n,)), pltpu.SemaphoreType.DMA((9,)), pltpu.SemaphoreType.DMA((H // 2, 2)),
+            pltpu.VMEM((T, D), BF),
+            pltpu.SemaphoreType.DMA((n,)), pltpu.SemaphoreType.DMA((n,)), pltpu.SemaphoreType.DMA((10,)), pltpu.SemaphoreType.DMA((H // 2, 2)),
         ],
         compiler_params=pltpu.CompilerParams(
             collective_id=0, has_side_effects=True, vmem_limit_bytes=60 << 20),

time: 211 us -> 210 us (level)
  no operation moved by 1% of the time
where the time goes in v2:
time: 210 us
  Pallas kernels  209 us (100%)
    pallas_call x1, Pallas kernels, third_call(): pl.pallas_call(third_kernel, in_specs=[SM] + [ANY] * 11 + [VM] * 2, out_s...  79.5 us
    pallas_call x1, Pallas kernels, first_call(): pl.pallas_call(first_kernel, in_specs=[S, ANY] + [V] * 12, out_specs=[ANY...  65.5 us
    pallas_call x1, Pallas kernels, second_call(): pl.pallas_call(second_kernel, in_specs=[SM] + [ANY] * 6 + [VM], out_specs...  59.7 us

profile of v2, /device:TPU:0, one launch (start us, length us, event | category | flops | bytes accessed | tf_op | source)
XLA Modules:
  0.0 210.0 jit_solution(16866468909385140911)
XLA Ops:
  1.3 65.5 %first_part.1 = (bf16[1024,768]{1,0:T(8,128)(2,1)}, bf16[1024,2304]{1,0:T(8,128)(2,1)}, bf16[1024,768]{1,0:T(8,128)(2,1)}, bf16[12,1024,128]{2,1,0:T(8,128)(2,1)...) custom-call(s32[1]{0:T(128)S(6)} %copy.29.length_ref, ...), custom_call_target="tpu_custom_call" | custom-call | tf_op jit(solution)/shard_map/first_part/pallas_call | solution.py:447
  66.8 59.7 %second_part.1 = (bf16[1024,768]{1,0:T(8,128)(2,1)}, bf16[1024,768]{1,0:T(8,128)(2,1)}, f32[1024,768]{1,0:T(8,128)}, bf16[768,3072]{1,0:T(8,128)(2,1)}, bf16[8,4...) custom-call(s32[1]{0:T(128)S(6)} %copy.29.length_ref, bf16[1024,768]{1,0:T(8,128)(2,1)} %x_hbm.3, ...), custom_call_target="tpu_custom_call" | custom-call | tf_op jit(solution)/shard_map/second_part/pallas_call | solution.py:1063
  126.5 79.5 %third_part.1 = (bf16[1024,768]{1,0:T(8,128)(2,1)}, f32[96,576]{1,0:T(8,128)}, f32[96,192]{1,0:T(8,128)}, f32[96,768]{1,0:T(8,128)}, f32[192,384]{1,0:T(8,128)}, /*index=5*/f32[8,384]{1,0:T(8,128)}) custom-call(s32[1]{0:T(128)S(6)} %copy.29.length_ref, bf16[1024,2304]{1,0:T(8,128)(2,1)} %get-tuple-element.56.proj_hbm, ...), custom_call_target="tpu_custom_call" | custom-call | tf_op jit(solution)/shard_map/third_part/pallas_call | solution.py:1381
  206.0 3.8 %last_part.1 = (bf16[1024,768]{1,0:T(8,128)(2,1)}, bf16[1024,768]{1,0:T(8,128)(2,1)}, f32[96,576]{1,0:T(8,128)}, f32[96,192]{1,0:T(8,128)}, f32[96,768]{1,0:T(8,...) custom-call(bf16[1024,768]{1,0:T(8,128)(2,1)} %get-tuple-element.55., ...), custom_call_target="tpu_custom_call" | custom-call | tf_op jit(solution)/shard_map/last_part/pallas_call | solution.py:1436
